TPU v7x, 512 devices: a whole 4x4x16 slice. The times are simulated.
512 devices in a mesh: energy: 64 (over y, z), slab: 8 (over x, core).
Axes of the slice: x: 4, y: 4, z: 16, core: 2. Of those that a mesh axis runs over, the one named last changes fastest.
Arguments:
- energies: float32 [64], P('energy'), may hold values from -1 to 1
- onsite: float32 [8, 256], P('slab'), may hold values from -1.5 to 1.5
- hopping: float32 [2, 8, 256, 256], P(None, 'slab'), may hold values from -0.09375 to 0.09375
- coupling: float32 [2, 8, 64, 64], P(None, 'slab'), may hold values from -0.1875 to 0.1875
- injection: float32 [64, 8, 256], P('energy', 'slab'), may hold values from 0.004 to 0.04
- kernels: float32 [2, 2, 127], replicated, may hold values from -0.75 to 0.75
Outputs:
- sigma_retarded: float32 [2, 8, 64, 256, 256], P(None, 'slab', None, 'energy')
- sigma_lesser: float32 [2, 8, 64, 256, 256], P(None, 'slab', None, 'energy')
All inputs are finite; a program needn't handle non-finite values.
Results may differ from a plain program's by a relative error of at most 0.0003.
Values sent between devices are 32-bit elements; how exact they have to be, the bound alone decides.
No kernel may reach another device: no remote copies, remote signals or barrier semaphores. Data moves between devices by JAX's collectives and lax.ppermute only.
A program may use at most 64 MiB of HBM per device.

v0:
```python
import functools

import jax
import jax.numpy as jnp
from jax import lax
from jax.experimental import pallas as pl
from jax.experimental.pallas import tpu as pltpu
from jax.sharding import PartitionSpec as P

ETA = 0.02
F32 = jnp.float32
BF16 = jnp.bfloat16
NN = (((1,), (0,)), ((), ()))
NT = (((1,), (1,)), ((), ()))


def mmh(a, b, dims=NN):
    return lax.dot_general(a, b, dims, precision=lax.Precision.HIGHEST, preferred_element_type=F32)


def halves(x):
    high = x.astype(BF16)
    return high, (x - high.astype(F32)).astype(BF16)


def mm1(a, b, dims=NN):
    return lax.dot_general(a, b, dims, preferred_element_type=F32)


def mm3(a, b, dims=NN):
    return mm1(a[0], b[0], dims) + (mm1(a[0], b[1], dims) + mm1(a[1], b[0], dims))


def mm(a, b, dims=NN):
    return mm3(halves(a), halves(b), dims)


def cat(parts, axis):
    return jnp.concatenate(parts, axis=axis)


def blk(r, i):
    return cat([cat([r, -i], 1), cat([i, r], 1)], 0)


def pair(z):
    n = z.shape[1] // 2
    return z[:n, :n], -z[:n, n:]


def full(top):
    n = top.shape[0]
    return cat([top, cat([-top[:, n:], top[:, :n]], 1)], 0)


def eye(n):
    return (lax.broadcasted_iota(jnp.int32, (n, n), 0) == lax.broadcasted_iota(jnp.int32, (n, n), 1)).astype(F32)


def imag_eye(n):
    return blk(jnp.zeros((n, n), F32), eye(n))


def times_i(z):
    n = z.shape[0] // 2
    return cat([-z[n:], z[:n]], 0)


def lowest(values):
    return functools.reduce(jnp.minimum, values)


def scaled(low, floor):
    base = jnp.maximum(low, floor)
    shift = 1.0 + base
    gain = 4.0 / (shift * shift)
    return shift, gain, jnp.minimum(gain * low * (shift - low), gain * base)


ENOUGH = 2e-4


def corrected(mats, xs):
    rs = [eye(z.shape[0]) - mmh(z, x) for z, x in zip(mats, xs)]
    size = functools.reduce(jnp.maximum, [jnp.sum(r * r) for r in rs])
    return size, tuple(x + mm1(x.astype(BF16), r.astype(BF16)) for x, r in zip(xs, rs))


def bound(z):
    zb = z.astype(BF16)
    w = mm1(zb, zb, NT)
    return 1.0 / (1.01 * jnp.max(jnp.sum(jnp.abs(w), axis=1, keepdims=True))), w, z.T


FLOOR = 0.035


def last_steps():
    low = FLOOR
    for _ in range(4):
        shift = 1.0 + low
        gain = 4.0 / (shift * shift)
        yield shift, gain
        low *= gain


def quick(sizes):
    def inverses(mats, factor=2.0):
        eyes = [eye(z.shape[0]) for z in mats]
        parts = [halves(z) for z in mats]
        shift = 1.0 + FLOOR
        gain = 4.0 / (shift * shift)
        lows, guesses = [], []
        for z, one in zip(mats, eyes):
            inv_u, w, zt = bound(z)
            r = shift * one - w * inv_u
            guesses.append(((gain * inv_u) * mm1(zt.astype(BF16), r.astype(BF16))).astype(BF16))
            lows.append((factor * ETA * ETA) * inv_u)
        low = lowest(lows)
        rise = gain * (shift - FLOOR)
        count = sum((low < FLOOR * rise**-k).astype(jnp.int32) for k in range(1, 20))

        def step(_, guesses):
            rs = [(shift * one - mm1(p[0], x)).astype(BF16) for p, one, x in zip(parts, eyes, guesses)]
            return tuple((gain * mm1(x, r)).astype(BF16) for x, r in zip(guesses, rs))

        guesses = lax.fori_loop(0, count, step, tuple(guesses))
        products = [mm1(zh, x) + mm1(zl, x) for (zh, zl), x in zip(parts, guesses)]
        for late, (late_shift, late_gain) in enumerate(last_steps()):
            rs = [(late_shift * one - y).astype(BF16) for one, y in zip(eyes, products)]
            if late < 3:
                both = [
                    late_gain * mm1(cat([x, y.astype(BF16)], 0), r) for x, y, r in zip(guesses, products, rs)
                ]
                guesses = [v[: v.shape[1]].astype(BF16) for v in both]
                products = [v[v.shape[1] :] for v in both]
            else:
                guesses = [(late_gain * mm1(x, r)).astype(BF16) for x, r in zip(guesses, rs)]
        better = []
        for (zh, zl), one, x in zip(parts, eyes, guesses):
            rh, rl = halves(one - (mm1(zh, x) + mm1(zl, x)))
            better.append(x.astype(F32) + (mm1(x, rh) + mm1(x, rl)))
        size, better = corrected(mats, better)
        sizes.append(size)
        return better

    return inverses


def careful(mats, factor=1.0):
    n = len(mats)
    eyes = [eye(z.shape[0]) for z in mats]
    parts = [halves(z) for z in mats]
    lows, xs = [], []
    for z in mats:
        inv_u, _, zt = bound(z)
        lows.append((ETA * ETA) * inv_u)
        xs.append(zt * inv_u)

    def step(state):
        lows, xs = state
        plans = [scaled(low, 1e-3) for low in lows]
        new = []
        for k in range(n):
            xp = halves(xs[k])
            r = plans[k][0] * eyes[k] - mm3(parts[k], xp)
            new.append(plans[k][1] * mm3(xp, halves(r)))
        return tuple(p[2] for p in plans), tuple(new)

    _, xs = lax.while_loop(lambda state: lowest(state[0]) < 0.999, step, (tuple(lows), tuple(xs)))

    def again(state):
        count, size, _ = state
        return (count < 8) & jnp.logical_not(size <= ENOUGH)

    def more(state):
        count, _, xs = state
        size, xs = corrected(mats, xs)
        return count + 1, size, xs

    size, xs = corrected(mats, xs)
    return lax.while_loop(again, more, (jnp.int32(0), size, xs))[2]


def guarded(run):
    sizes = []
    run(quick(sizes))

    @pl.when(jnp.logical_not(functools.reduce(jnp.maximum, sizes) <= ENOUGH))
    def _():
        run(careful)


def rolled(x, axis):
    n = x.shape[axis]
    if axis == 0:
        return cat([x[n - 64 :], x[: n - 64]], 0)
    return cat([x[:, n - 64 :], x[:, : n - 64]], 1)


def unrolled(x, axis):
    if axis == 0:
        return cat([x[64:], x[:64]], 0)
    return cat([x[:, 64:], x[:, :64]], 1)


def eliminate_body(inverses, detune, hop):
    h0 = rolled(rolled(hop[0], 0), 1)
    h1 = rolled(rolled(hop[1], 0), 1)
    one = eye(256)
    ar = one * rolled(detune, 1) - (h0 + h0.T) * 0.5
    ai = one * ETA - (h1 - h1.T) * 0.5

    def part(rows, cols):
        return blk(ar[rows, cols], ai[rows, cols])

    b, i = slice(0, 128), slice(128, 256)
    (inner,) = inverses([part(i, i)], 1.0)
    abi = part(b, i)
    y = mm(abi, inner)
    z = mm(inner, part(i, b))
    s = part(b, b) - mm(abi, z)
    return s, inner[:128], y, z[:128]


def corners(s):
    r, i = pair(s)
    lo, hi = slice(0, 64), slice(64, 128)
    return [[blk(r[p, q], i[p, q]) for q in (lo, hi)] for p in (lo, hi)]


def lead_of(slab, c):
    return jnp.where(slab == 0, mm(c, c, NT), 0.0)


def maps_body(inverses, slab, s, couple, next_couple):
    (bb, bf), (fb, ff) = corners(s)
    c = blk(couple[0], couple[1])
    cn = blk(next_couple[0], next_couple[1])
    ff = ff + times_i(lead_of(slab, c))
    ib, if_ = inverses([bb, ff])
    b = -mm(ib, bf)
    d = -mm(fb, ib)
    phi = ff + mm(d, bf)
    br = -mm(if_, fb)
    dr = -mm(bf, if_)
    psi = bb + mm(dr, fb)
    ct = c.T
    cnt = cn.T
    left = [mm(mm(cn, ib), cnt), mm(cn, b), mm(d, cnt), phi]
    right = [mm(mm(ct, if_), c), mm(ct, br), mm(dr, c), psi]
    raw = [ib, b, d, phi]
    return [u[:64] for u in left], [u[:64] for u in right], [u[:64] for u in raw]


def compose(outer, inner, phi_inv):
    a2, b2, d2, _ = outer
    a1, b1, d1, phi1 = inner
    pq = mm(phi_inv, cat([b1, d2], 1))
    quad = mm(cat([b2, d1], 0), pq)
    n = a1.shape[0]
    return [a2 + quad[:n, n:], quad[:n, :n], quad[n:, n:], phi1 - quad[n:, :n]]


def level(inverses, slots):
    phis = inverses([outer[3] - inner[0] for outer, inner in slots])
    return [[u[:64] for u in compose(o, i, p)] for (o, i), p in zip(slots, phis)]


def constant_map(value):
    zero = jnp.zeros_like(value)
    return [value, zero, zero, imag_eye(64)]


def choose(cond, one, other):
    return [jnp.where(cond, x, y) for x, y in zip(one, other)]


def tree_body(inverses, slab, sent, put, get):
    none = constant_map(jnp.zeros((128, 128), F32))

    def wide(tops):
        return [full(u) for u in tops]

    lefts = (slab + 1) // 2

    def fetch(is_left, place):
        source = jnp.where(is_left, slab - 1 - place, slab + 1 + place)
        there = (source >= 0) & (source < 8)
        return choose(there, wide(sent(jnp.clip(source, 0, 7))), none)

    slots = []
    for k in range(4):
        is_left = k < lefts
        place = 2 * jnp.where(is_left, k, k - lefts)
        slots.append((fetch(is_left, place), fetch(is_left, place + 1)))
    for k, m in enumerate(level(inverses, slots)):
        put(k, m)

    skip = jnp.where(lefts == 1, 1, 0)
    last = choose(lax.rem(lefts, 2) == 0, wide(get(3)), none)
    slots = [(wide(get(skip)), wide(get(skip + 1))), (wide(get(skip + 2)), last)]
    for k, m in enumerate(level(inverses, slots)):
        put(4 + k, m)

    second = wide(get(5))
    left = choose(lefts == 0, none, wide(get(jnp.where(lefts == 1, 0, 4))))
    right = choose(lefts == 4, none, wide(get(jnp.where(lefts == 3, 3, jnp.where(lefts == 2, 5, 4)))))
    slots = [(left, choose(lefts >= 3, second, none)), (right, choose(lefts <= 1, second, none))]
    phis = inverses([outer[3] - inner[0] for outer, inner in slots])
    return [o[0] + mm(mm(o[1], p), o[2]) for (o, _), p in zip(slots, phis)]


def close_body(inverses, slab, couple, sig_l, sig_r, s, inner, y, z, raw):
    ib, b, d, phi = [full(u) for u in raw]
    lr, li = pair(sig_l - times_i(lead_of(slab, blk(couple[0], couple[1]))))
    rr, ri = pair(sig_r)
    zero = jnp.zeros((64, 64), F32)

    def spread(x, w):
        return cat([cat([x, zero], 1), cat([zero, w], 1)], 0)

    closed = s - blk(spread(rr, lr), spread(ri, li))
    e_inv, big = inverses([phi - sig_l, closed])
    be = mm(b, e_inv)
    gfb = mm(e_inv, d)
    gbb = ib + mm(be, d)

    def joined(k):
        return cat([cat([pair(gbb)[k], pair(be)[k]], 1), cat([pair(gfb)[k], pair(e_inv)[k]], 1)], 0)

    small = cat([joined(0), -joined(1)], 1)
    return big[:128], small


def restore(top, inner, y, z):
    ty = mm(top, y)
    zt = mm(z, full(top))
    zty = mm(zt, y)
    low = inner + zty
    r = cat([cat([top[:, :128], -ty[:, :128]], 1), cat([-zt[:, :128], low[:, :128]], 1)], 0)
    i = cat([cat([-top[:, 128:], ty[:, 128:]], 1), cat([zt[:, 128:], -low[:, 128:]], 1)], 0)
    return r, i


def for_rows(r, i):
    r, i = [unrolled(unrolled(x, 0), 1).reshape(32, 8, 256) for x in (r, i)]
    upper = lax.broadcasted_iota(jnp.int32, (32, 8, 256), 1) < 4

    def swapped(x):
        return cat([x[:, 4:], x[:, :4]], 1)

    even = jnp.where(upper, r, swapped(i))
    odd = jnp.where(upper, swapped(r), i)
    return even, odd


def right_adj(lr, li, gr, gi):
    n = lr.shape[0]
    rows = cat([cat([lr, li], 1), cat([li, -lr], 1)], 0)
    out = mm(rows, cat([gr, gi], 1), NT)
    return out[:n], out[n:]


def lesser_parts_body(slab, big, small, y, inject, couple, next_couple):
    rest = mm(cat([small, big], 0), y)
    gr, gi = cat([small[:, :128], -rest[:128, :128]], 1), cat([-small[:, 128:], rest[:128, 128:]], 1)
    fr, fi = cat([big[:, :128], -rest[128:, :128]], 1), cat([-big[:, 128:], rest[128:, 128:]], 1)
    hr, hi = 1.5 * gr - fr, 1.5 * gi - fi
    d = rolled(inject, 1)
    lr = cat([gr[:64], hr[64:]], 0) * d
    li = cat([gi[:64], hi[64:]], 0) * d
    mr, mi = right_adj(lr, li, gr, gi)
    c = blk(couple[0], couple[1])
    cn = blk(next_couple[0], next_couple[1])
    ct, cnt = c.T, cn.T
    w = mm(mm(cn, blk(-mi[:64, :64], mr[:64, :64])), cnt)
    beta = mm(cn, blk(gr[:64, 64:128], gi[:64, 64:128]))
    w = w + mm(mm(beta, times_i(lead_of(slab, c))), beta, NT)
    w = (w - w.T) * 0.5
    q = mm(mm(ct, blk(-mi[64:, 64:], mr[64:, 64:])), c)
    q = q - q.T
    left = mm(
        ct,
        cat(
            [
                blk(gr[64:128, 64:128], gi[64:128, 64:128]),
                blk(hr[64:128, 64:128], hi[64:128, 64:128]),
                blk(gr[64:128, :64], gi[64:128, :64]),
            ],
            1,
        ),
    )
    u, v, zz = left[:, :128], left[:, 128:256], left[:, 256:]
    return [m[:64] for m in (w + times_i(q), beta, u, v, zz)]


def lesser_body(slab, couple, parts, big, small, inner, y, z, inject):
    mine = times_i(lead_of(slab, blk(couple[0], couple[1])))
    sources = {}
    packed = [full(parts(t, 0)) for t in range(8)]
    for t in range(8):
        if t:
            beta = full(parts(t - 1, 1))
            both = packed[t - 1]
            w = (both - both.T) * 0.5
            sig = w + mm(mm(beta, sig), beta, NT) if t > 1 else w
            mine = jnp.where(slab == t, sig, mine)
            c = mm(mm(full(parts(t, 3)), sig), full(parts(t, 2)), NT)
            sources[t] = c - c.T - times_i((packed[t] + packed[t].T) * 0.5)
    back = jnp.zeros_like(sig)
    my_back = back
    for t in range(7, 0, -1):
        zz = full(parts(t, 4))
        back = sources[t] + mm(mm(zz, back), zz, NT)
        my_back = jnp.where(slab == t - 1, back, my_back)
    gr, gi = restore(small, inner, y, z)
    fr, fi = restore(big, inner, y, z)
    hr, hi = 1.5 * gr - fr, 1.5 * gi - fi
    d = rolled(inject, 1)
    right_r, right_i = pair(mine)
    back_r, back_i = pair(0.5 * my_back)

    def cols(xr, xi, m):
        out = mm(cat([xr, xi], 1), m)
        return out

    fm = cat([cat([right_r, right_i], 1), cat([-right_i, right_r], 1)], 0)
    bm = cat([cat([back_r, back_i], 1), cat([-back_i, back_r], 1)], 0)
    on_f = cols(hr[:, 64:128], hi[:, 64:128], fm)
    on_b = cols(gr[:, :64], gi[:, :64], bm)
    add_r = cat([on_b[:, :64], on_f[:, :64]], 1)
    add_i = cat([on_b[:, 64:], on_f[:, 64:]], 1)
    lr, li = -hi * d, hr * d
    lr = cat([lr[:, :128] + add_r, lr[:, 128:]], 1)
    li = cat([li[:, :128] + add_i, li[:, 128:]], 1)
    nr, ni = right_adj(lr, li, gr, gi)
    return nr - nr.T, ni + ni.T


VM = pl.BlockSpec(memory_space=pltpu.VMEM)
SM = pl.BlockSpec(memory_space=pltpu.SMEM)


def call(kernel, outs, specs, micros, scratch=()):
    return pl.pallas_call(
        kernel,
        out_shape=[jax.ShapeDtypeStruct(o, F32) for o in outs],
        in_specs=specs,
        out_specs=[VM] * len(outs),
        scratch_shapes=list(scratch),
        compiler_params=pltpu.CompilerParams(vmem_limit_bytes=40 * 2**20),
        cost_estimate=pl.CostEstimate(flops=int(micros * 1.1e9), bytes_accessed=1 << 20, transcendentals=0),
    )


def put(ref, values):
    for k, v in enumerate(values):
        ref[k] = v


def eliminate_kernel(detune, hop, s, inner, y, z):
    def run(inverses):
        s[...], inner[...], y[...], z[...] = eliminate_body(inverses, detune[...], (hop[0, 0], hop[1, 0]))

    guarded(run)


def maps_kernel(slab, s, couple, next_couple, sends, raw):
    chip, core = slab[0] // 2, lax.rem(slab[0], 2)

    def run(inverses):
        left, right, own = maps_body(inverses, slab[0], s[...], (couple[0, 0], couple[1, 0]), (next_couple[0, 0], next_couple[1, 0]))
        put(raw, own)
        for t in range(4):
            put(sends.at[t], choose((chip < t) | ((chip == t) & (core == 0)), left, right))

    guarded(run)


def put_rows(ref, r, i):
    even, odd = for_rows(r, i)
    ref[:, 0] = even
    ref[:, 1] = odd


def close_kernel(
    slab, couple, next_couple, inject, near, far, s, inner, y, z, raw, rows, big, small, parts, kept
):
    me = slab[0]
    own_couple = (couple[0, 0], couple[1, 0])

    def sent(t):
        same = lax.rem(t, 2) == lax.rem(me, 2)
        return [jnp.where(same, near[t // 2, k], far[t // 2, k]) for k in range(4)]

    def run(inverses):
        def get(t):
            return [kept[t, k] for k in range(4)]

        sig_l, sig_r = tree_body(inverses, me, sent, lambda k, m: put(kept.at[k], m), get)
        own = [raw[k] for k in range(4)]
        whole, corner = close_body(
            inverses, me, own_couple, sig_l, sig_r, s[...], inner[...], y[...], z[...], own
        )
        big[...], small[...] = whole, corner
        put(parts, lesser_parts_body(me, whole, corner, y[...], inject[:, 0], own_couple, (next_couple[0, 0], next_couple[1, 0])))
        put_rows(rows, *restore(whole, inner[...], y[...], z[...]))

    guarded(run)


def lesser_kernel(slab, couple, parts, big, small, inner, y, z, inject, rows):
    r, i = lesser_body(
        slab[0],
        (couple[0, 0], couple[1, 0]),
        lambda t, k: parts[t, k],
        big[...],
        small[...],
        inner[...],
        y[...],
        z[...],
        inject[:, 0],
    )
    put_rows(rows, r, i)


def convolve_kernel(table, piece, out):
    for j in range(4):
        x = cat([piece[:, j], piece[:, 4 + j]], 0)
        o = mm(table[...], x)
        out[0, 0, :, j] = o[:64]
        out[1, 0, :, j] = o[64:]


def tables_kernel(kern, out):
    for k in range(2):
        t = []
        for c in range(2):
            x = jnp.broadcast_to(kern[k, c : c + 1, :], (64, 128))
            t.append(pltpu.roll(x, 65, 1, stride=1, stride_axis=0)[:, :64])
        out[k] = blk(t[0], t[1])


def per_device(energies, onsite, hopping, coupling, injection, kernels):
    slab = lax.axis_index("slab").astype(jnp.int32).reshape(1)

    def swapped_over(x, axis):
        return lax.all_to_all(x, axis, split_axis=0, concat_axis=0, tiled=True)

    next_couple = lax.ppermute(coupling, "slab", [(t, (t + 7) % 8) for t in range(8)])
    m256, half = (256, 256), (128, 256)
    port = (4, 64, 128)
    s, inner, y, z = call(eliminate_kernel, [m256, half, m256, half], [VM, VM], 6)(energies[:, None] - onsite, hopping)
    sends, raw = call(maps_kernel, [(4, *port), port], [SM] + [VM] * 3, 5)(slab, s, coupling, next_couple)
    near = lax.all_to_all(
        sends, "slab", split_axis=0, concat_axis=0, tiled=True, axis_index_groups=[[0, 2, 4, 6], [1, 3, 5, 7]]
    )
    far = lax.ppermute(near, "slab", [(t, t ^ 1) for t in range(8)])
    rows, big, small, parts = call(
        close_kernel,
        [(32, 2, 8, 256), half, half, (5, 64, 128)],
        [SM] + [VM] * 10,
        25,
        [pltpu.VMEM((6, 4, 64, 128), F32)],
    )(slab, coupling, next_couple, injection, near, far, s, inner, y, z, raw)

    def to_rows(x):
        return swapped_over(x.reshape(64, 8, 256), "energy")

    got_r = to_rows(rows)
    all_parts = lax.all_gather(parts, "slab")
    late_kernels, _ = lax.optimization_barrier((kernels, parts))
    reversed_kernels = jnp.pad(late_kernels[:, :, ::-1], ((0, 0), (0, 0), (0, 1)))
    (tables,) = call(tables_kernel, [(2, 128, 128)], [VM], 1)(reversed_kernels)
    (rows_l,) = call(lesser_kernel, [(32, 2, 8, 256)], [SM] + [VM] * 8, 8)(
        slab, coupling, all_parts, big, small, inner, y, z, injection
    )
    got_l = to_rows(rows_l)
    conv = call(convolve_kernel, [(2, 1, 64, 4, 256)], [VM] * 2, 2)
    return conv(tables[0], got_r)[0], conv(tables[1], got_l)[0]


def solution(mesh):
    in_specs = (
        P("energy"),
        P("slab", None),
        P(None, "slab", None, None),
        P(None, "slab", None, None),
        P("energy", "slab", None),
        P(),
    )
    out_specs = (P(None, "slab", None, "energy", None), P(None, "slab", None, "energy", None))
    return jax.shard_map(per_device, mesh=mesh, in_specs=in_specs, out_specs=out_specs, check_vma=False)
```

profile of v0, /device:TPU:1, one launch (start us, length us, event | category | flops | bytes accessed | tf_op | source)
XLA Modules:
  0.0 190.3 jit_solution(12930655240701452906)
XLA Ops:
  7.2 0.0 all-gather.3.cloned.1.call-start
  7.2 6.9 %collective-permute-start = (f32[2,1,64,64]{3,2,1,0:T(8,128)}, f32[2,1,64,64]{3,2,1,0:T(8,128)S(1)}, u32[]{:S(2)}, u32[]{:S(2)}) collective-permute-start(f32[2,1,64,64]{3,2,1,0:T(8,128)} %couple.5), channel_id=1, source_target_pairs={{0,7},{1,0},{2,1},{3,2},{4,3},{5,4},{6,5},{7,6},{8,15},{9,8},{10,9... | collective-permute-start | bytes 98312 | tf_op jit(solution)/shard_map/ppermute | solution.py:551
  14.7 0.7 broadcast_subtract_fusion.detune
  15.4 0.0 copy-start.1
  15.4 1.0 copy-done.1
  16.5 0.0 copy-start.2
  16.5 5.7 %shard_map.77 = (f32[256,256]{1,0:T(8,128)S(1)}, f32[128,256]{1,0:T(8,128)S(1)}, f32[256,256]{1,0:T(8,128)S(1)}, f32[128,256]{1,0:T(8,128)S(1)}) custom-call(f32[1,256]{1,0:T(1,128)S(1)} %broadcast_subtract_fusion.detune, f32[2,1,256,256]{3,2,1,0:T(8,128)S(1)} %copy-done.1), custom_call_target="tpu_custom_call" | custom-call | flops 6600000000 | bytes 1048576 | tf_op jit(solution)/shard_map/pallas_call | solution.py:554
  22.2 0.0 collective-permute-done.next_couple
  22.2 0.0 copy-done.2
  22.2 0.0 copy-start.3
  22.2 4.3 %shard_map.78 = (f32[4,4,64,128]{3,2,1,0:T(8,128)S(1)}, f32[4,64,128]{2,1,0:T(8,128)S(1)}) custom-call(s32[1]{0:T(128)} %bitcast.slab, f32[256,256]{1,0:T(8,128)S(1)} %get-tuple-element.13.s, f32[2,1,64,64]{3,2,1,0:T(8,128)S(1)} %copy-done.2, f32[2,1,64,64]{3,2,1,0:T(8,128)S(1)} %collective-permute-done.next_couple), custom_call_target="tpu_custom_call" | custom-call | flops 5500000256 | bytes 1048576 | tf_op jit(solution)/shard_map/pallas_call | solution.py:555
  26.5 11.7 %all_to_all.15.near = f32[4,4,64,128]{3,2,1,0:T(8,128)S(1)} all-to-all(f32[4,4,64,128]{3,2,1,0:T(8,128)S(1)} %get-tuple-element.14), channel_id=1, replica_groups={{0,2,4,6},{1,3,5,7},{8,10,12,14},{9,11,13,15},{16,18,20,22},{17,19,21,2..., dimensions={0} | all-to-all | bytes 1048576 | tf_op jit(solution)/shard_map/all_to_all | solution.py:556
  38.3 3.0 %collective-permute-start.1 = (f32[4,4,64,128]{3,2,1,0:T(8,128)S(1)}, f32[4,4,64,128]{3,2,1,0:T(8,128)S(1)}, u32[]{:S(2)}, u32[]{:S(2)}) collective-permute-start(f32[4,4,64,128]{3,2,1,0:T(8,128)S(1)} %all_to_all.15.near), channel_id=1, source_target_pairs={{0,1},{1,0},{2,3},{3,2},{4,5},{5,4},{6,7},{7,6},{8,9},{9,8},{10,11... | collective-permute-start | bytes 1572872 | tf_op jit(solution)/shard_map/ppermute | solution.py:559
  41.2 1.5 collective-permute-done.1.far
  42.8 0.0 copy-done.3
  42.8 23.1 %shard_map.79 = (f32[32,2,8,256]{3,2,1,0:T(8,128)}, f32[128,256]{1,0:T(8,128)S(1)}, f32[128,256]{1,0:T(8,128)S(1)}, f32[5,64,128]{2,1,0:T(8,128)}) custom-call(s32[1]{0:T(128)} %bitcast.slab, f32[2,1,64,64]{3,2,1,0:T(8,128)S(1)} %copy-done.2, f32[2,1,64,64]{3,2,1,0:T(8,128)S(1)} %collective-permute-done.next_couple, f32[1,1,256]{2,1,0:T(1,128)S(1)} %copy-done.3, ...), custom_call_target="tpu_custom_call" | custom-call | flops 27499999232 | bytes 1048576 | tf_op jit(solution)/shard_map/pallas_call | solution.py:560
  65.8 0.0 all-gather.3.cloned.1.call-update
  65.8 15.3 %all-to-all-start.1 = ((f32[64,8,256]{2,1,0:T(8,128)}), f32[64,8,256]{2,1,0:T(8,128)S(1)}, u32[]{:S(2)}, u32[]{:S(2)}) async-start(f32[64,8,256]{2,1,0:T(8,128)} %bitcast.3), calls=%async_computation.1 | async-start | bytes 1048576 | tf_op jit(solution)/shard_map/all_to_all | solution.py:549
  81.2 46.7 %all-gather.3.cloned.1.call-done = f32[40,64,128]{2,1,0:T(8,128)} async-done(((f32[5,64,128]{2,1,0:T(8,128)}), f32[40,64,128]{2,1,0:T(8,128)}) %all-gather.3.cloned.1.call-update) | async-done | bytes 1310736 | tf_op jit(solution)/shard_map/all_gather | solution.py:572
  127.9 0.0 copy-start
  127.9 1.3 copy-done
  129.2 0.0 copy-start.4
  129.2 7.5 %shard_map.82 = f32[32,2,8,256]{3,2,1,0:T(8,128)} custom-call(s32[1]{0:T(128)} %bitcast.slab, f32[2,1,64,64]{3,2,1,0:T(8,128)S(1)} %copy-done.2, f32[8,5,64,128]{3,2,1,0:T(8,128)S(1)} %bitcast.10, f32[128,256]{1,0:T(8,128)S(1)} %get-tuple-element.22.big, f32[128,256]{1,0:T(8,128)S(1)} %get-tuple-element.23.small, f32[128,256]{1,0:T(8,128)S(1)} %get-tuple-element.15.inner, ...), custom_call_target="tpu_custom_call" | custom-call | flops 8800000000 | bytes 1048576 | tf_op jit(solution)/shard_map/pallas_call | solution.py:576
  136.8 0.0 all-to-all-done.1.piece
  136.8 15.4 %all-to-all-start.2 = ((f32[64,8,256]{2,1,0:T(8,128)}), f32[64,8,256]{2,1,0:T(8,128)S(1)}, u32[]{:S(2)}, u32[]{:S(2)}) async-start(f32[64,8,256]{2,1,0:T(8,128)} %bitcast.6), calls=%async_computation.2 | async-start | bytes 1048576 | tf_op jit(solution)/shard_map/all_to_all | solution.py:549
  152.1 0.0 copy-done.4
  152.1 0.1 rev.3
  152.2 0.2 shard_map.80
  152.5 1.3 shard_map.81
  153.8 28.4 %all-to-all-done.2.piece = f32[64,8,256]{2,1,0:T(8,128)S(1)} async-done(((f32[64,8,256]{2,1,0:T(8,128)}), f32[64,8,256]{2,1,0:T(8,128)S(1)}, u32[]{:S(2)}, u32[]{:S(2)}) %all-to-all-start.2) | async-done | bytes 524320 | tf_op jit(solution)/shard_map/all_to_all | solution.py:549
  182.2 1.3 shard_map.83
  (2 shorter events, 0.0 us)
Async XLA Ops:
  7.2 120.7 %all-gather.3.cloned.1.call-start = ((), (), s32[]{:S(2)}) async-start(), calls=%async_computation.3 | async-start | bytes 1474560 | tf_op jit(solution)/shard_map/all_gather | solution.py:572
  7.2 15.0 %collective-permute-start = (f32[2,1,64,64]{3,2,1,0:T(8,128)}, f32[2,1,64,64]{3,2,1,0:T(8,128)S(1)}, u32[]{:S(2)}, u32[]{:S(2)}) collective-permute-start(f32[2,1,64,64]{3,2,1,0:T(8,128)} %couple.5), channel_id=1, source_target_pairs={{0,7},{1,0},{2,1},{3,2},{4,3},{5,4},{6,5},{7,6},{8,15},{9,8},{10,9... | collective-permute-start | bytes 98312 | tf_op jit(solution)/shard_map/ppermute | solution.py:551
  15.4 1.0 copy-start.1
  16.5 5.7 %copy-start.2 = (f32[2,1,64,64]{3,2,1,0:T(8,128)S(1)}, f32[2,1,64,64]{3,2,1,0:T(8,128)}, u32[]{:S(2)}) copy-start(f32[2,1,64,64]{3,2,1,0:T(8,128)} %couple.5) | copy-start | bytes 98308
  22.2 20.6 %copy-start.3 = (f32[1,1,256]{2,1,0:T(1,128)S(1)}, f32[1,1,256]{2,1,0:T(1,128)}, u32[]{:S(2)}) copy-start(f32[1,1,256]{2,1,0:T(1,128)} %inject.3) | copy-start | bytes 3076
  38.3 4.5 %collective-permute-start.1 = (f32[4,4,64,128]{3,2,1,0:T(8,128)S(1)}, f32[4,4,64,128]{3,2,1,0:T(8,128)S(1)}, u32[]{:S(2)}, u32[]{:S(2)}) collective-permute-start(f32[4,4,64,128]{3,2,1,0:T(8,128)S(1)} %all_to_all.15.near), channel_id=1, source_target_pairs={{0,1},{1,0},{2,3},{3,2},{4,5},{5,4},{6,7},{7,6},{8,9},{9,8},{10,11... | collective-permute-start | bytes 1572872 | tf_op jit(solution)/shard_map/ppermute | solution.py:559
  65.8 70.9 %all-to-all-start.1 = ((f32[64,8,256]{2,1,0:T(8,128)}), f32[64,8,256]{2,1,0:T(8,128)S(1)}, u32[]{:S(2)}, u32[]{:S(2)}) async-start(f32[64,8,256]{2,1,0:T(8,128)} %bitcast.3), calls=%async_computation.1 | async-start | bytes 1048576 | tf_op jit(solution)/shard_map/all_to_all | solution.py:549
  127.9 1.3 copy-start
  129.2 22.9 %copy-start.4 = (f32[2,2,127]{2,1,0:T(2,128)S(1)}, f32[2,2,127]{2,1,0:T(2,128)}, u32[]{:S(2)}) copy-start(f32[2,2,127]{2,1,0:T(2,128)} %param.11) | copy-start | bytes 6100
  136.8 45.4 %all-to-all-start.2 = ((f32[64,8,256]{2,1,0:T(8,128)}), f32[64,8,256]{2,1,0:T(8,128)S(1)}, u32[]{:S(2)}, u32[]{:S(2)}) async-start(f32[64,8,256]{2,1,0:T(8,128)} %bitcast.6), calls=%async_computation.2 | async-start | bytes 1048576 | tf_op jit(solution)/shard_map/all_to_all | solution.py:549
Sparse Core Ops, SparseCore 0:
  66.0 61.8 all-gather.2
where the time goes:
time: 192 us; the launch traced here: 190 us
  waiting for transfers between devices  76.6 us (40%)
  Pallas kernels  43.4 us (23%)
  starting transfers between devices  40.6 us (21%)
  between operations  14.8 us (8%)
  blocking collectives  11.7 us (6%)
  local copies, waits for them, and re-layouts  2.49 us (1%)
    all_gather x1, waiting for transfers between devices, per_device(): all_parts = lax.all_gather(parts, 'slab')  46.7 us
    all_to_all x2, starting transfers between devices, swapped_over(): return lax.all_to_all(x, axis, split_axis=0, concat_axis=0, tiled=True)  30.7 us
    all_to_all x2, waiting for transfers between devices, swapped_over(): return lax.all_to_all(x, axis, split_axis=0, concat_axis=0, tiled=True)  28.4 us
    pallas_call x1, Pallas kernels, per_device(): call(close_kernel, [(32, 2, 8, 256), half, half, (5, 64, 128)], [SM] + [V...  23.1 us
    all_to_all x1, blocking collectives, per_device(): lax.all_to_all(sends, 'slab', split_axis=0, concat_axis=0, tiled=True, ax...  11.7 us
    pallas_call x1, Pallas kernels, per_device(): call(lesser_kernel, [(32, 2, 8, 256)], [SM] + [VM] * 8, 8)  7.53 us
    ppermute x1, starting transfers between devices, per_device(): lax.ppermute(coupling, 'slab', [(t, (t + 7) % 8) for t in range(8)])  6.89 us
    pallas_call x1, Pallas kernels, per_device(): call(eliminate_kernel, [m256, half, m256, half], [VM, VM], 6)  5.7 us
  transfers between devices with their start and end apart: 5, of which 3 were waited for; matrix products, arithmetic and copies ran while one was open for 0% of the time, Pallas kernels for 8%

commit v1 on v0

--- a/solution.py
+++ b/solution.py
@@ -510,11 +510,17 @@
     guarded(run)
 
 
-def lesser_kernel(slab, couple, parts, big, small, inner, y, z, inject, rows):
+def lesser_kernel(slab, couple, near, far, big, small, inner, y, z, inject, rows):
+    me = slab[0]
+
+    def parts(t, k):
+        d = lax.rem(t // 2 - me // 2 + 4, 4)
+        return jnp.where(lax.rem(me, 2) == t % 2, near[d, k], far[d, k])
+
     r, i = lesser_body(
-        slab[0],
+        me,
         (couple[0, 0], couple[1, 0]),
-        lambda t, k: parts[t, k],
+        parts,
         big[...],
         small[...],
         inner[...],
@@ -569,12 +575,15 @@
         return swapped_over(x.reshape(64, 8, 256), "energy")
 
     got_r = to_rows(rows)
-    all_parts = lax.all_gather(parts, "slab")
+    near_parts = jnp.stack(
+        [parts] + [lax.ppermute(parts, "slab", [(t, (t - 2 * d) % 8) for t in range(8)]) for d in (1, 2, 3)]
+    )
+    far_parts = lax.ppermute(near_parts, "slab", [(t, t ^ 1) for t in range(8)])
     late_kernels, _ = lax.optimization_barrier((kernels, parts))
     reversed_kernels = jnp.pad(late_kernels[:, :, ::-1], ((0, 0), (0, 0), (0, 1)))
     (tables,) = call(tables_kernel, [(2, 128, 128)], [VM], 1)(reversed_kernels)
-    (rows_l,) = call(lesser_kernel, [(32, 2, 8, 256)], [SM] + [VM] * 8, 8)(
-        slab, coupling, all_parts, big, small, inner, y, z, injection
+    (rows_l,) = call(lesser_kernel, [(32, 2, 8, 256)], [SM] + [VM] * 9, 8)(
+        slab, coupling, near_parts, far_parts, big, small, inner, y, z, injection
     )
     got_l = to_rows(rows_l)
     conv = call(convolve_kernel, [(2, 1, 64, 4, 256)], [VM] * 2, 2)

time: 192 us -> 183 us (0.953)
  starting transfers between devices: 40.6 us -> 82.6 us
  waiting for transfers between devices: 76.6 us -> 37 us
  between operations: 14.8 us -> 1.42 us
    all_gather x1 -> x0, waiting for transfers between devices: 46.7 us -> none  [per_device(): all_parts = lax.all_gather(parts, 'slab')]
    all_to_all x2, starting transfers between devices: 30.7 us -> 60.6 us  [swapped_over(): return lax.all_to_all(x, axis, split_axis=0, concat_axis=0, tiled=True)]
    ppermute x0 -> x4, starting transfers between devices: none -> 11.9 us  [the longest x3 8.52 us: per_device(): lax.ppermute(parts, 'slab', [(t, (t - 2 * d) % 8) for t in range(8)])]
    ppermute x0 -> x4, waiting for transfers between devices: none -> 7.36 us  [the longest x3 5.66 us: per_device(): lax.ppermute(parts, 'slab', [(t, (t - 2 * d) % 8) for t in range(8)])]
  transfers between devices with their start and end apart: 5 -> 8, of which waited for: 3 -> 6; matrix products, arithmetic and copies ran while one was open for 0% -> 0% of each run, Pallas kernels for 8% -> 8%
where the time goes in v1:
time: 183 us; the launch traced here: 180 us
  starting transfers between devices  82.6 us (45%)
  Pallas kernels  44.7 us (24%)
  waiting for transfers between devices  37 us (20%)
  blocking collectives  11.6 us (6%)
  local copies, waits for them, and re-layouts  2.51 us (1%)
    all_to_all x2, starting transfers between devices, swapped_over(): return lax.all_to_all(x, axis, split_axis=0, concat_axis=0, tiled=True)  60.6 us
    all_to_all x2, waiting for transfers between devices, swapped_over(): return lax.all_to_all(x, axis, split_axis=0, concat_axis=0, tiled=True)  28.1 us
    pallas_call x1, Pallas kernels, per_device(): call(close_kernel, [(32, 2, 8, 256), half, half, (5, 64, 128)], [SM] + [V...  24.4 us
    all_to_all x1, blocking collectives, per_device(): lax.all_to_all(sends, 'slab', split_axis=0, concat_axis=0, tiled=True, ax...  11.6 us
    ppermute x3, starting transfers between devices, per_device(): lax.ppermute(parts, 'slab', [(t, (t - 2 * d) % 8) for t in range(8)])  8.52 us
    pallas_call x1, Pallas kernels, per_device(): call(lesser_kernel, [(32, 2, 8, 256)], [SM] + [VM] * 9, 8)  7.54 us
    ppermute x1, starting transfers between devices, per_device(): lax.ppermute(coupling, 'slab', [(t, (t + 7) % 8) for t in range(8)])  6.89 us
    pallas_call x1, Pallas kernels, per_device(): call(eliminate_kernel, [m256, half, m256, half], [VM, VM], 6)  5.71 us
  transfers between devices with their start and end apart: 8, of which 6 were waited for; matrix products, arithmetic and copies ran while one was open for 0% of the time, Pallas kernels for 8%

profile of v1, /device:TPU:1, one launch (start us, length us, event | category | flops | bytes accessed | tf_op | source)
XLA Modules:
  0.0 179.8 jit_solution(3461803913740471998)
XLA Ops:
  0.6 6.9 %collective-permute-start = (f32[2,1,64,64]{3,2,1,0:T(8,128)}, f32[2,1,64,64]{3,2,1,0:T(8,128)S(1)}, u32[]{:S(2)}, u32[]{:S(2)}) collective-permute-start(f32[2,1,64,64]{3,2,1,0:T(8,128)} %couple.5), channel_id=1, source_target_pairs={{0,7},{1,0},{2,1},{3,2},{4,3},{5,4},{6,5},{7,6},{8,15},{9,8},{10,9... | collective-permute-start | bytes 98312 | tf_op jit(solution)/shard_map/ppermute | solution.py:557
  8.2 0.0 copy-start.4
  8.2 0.7 copy-done.4
  8.9 0.0 copy-start
  8.9 1.0 copy-done
  9.9 5.7 %shard_map.77 = (f32[256,256]{1,0:T(8,128)S(1)}, f32[128,256]{1,0:T(8,128)S(1)}, f32[256,256]{1,0:T(8,128)S(1)}, f32[128,256]{1,0:T(8,128)S(1)}) custom-call(f32[1,256]{1,0:T(1,128)S(1)} %broadcast_subtract_fusion.detune, f32[2,1,256,256]{3,2,1,0:T(8,128)S(1)} %copy-done), custom_call_target="tpu_custom_call" | custom-call | flops 6600000000 | bytes 1048576 | tf_op jit(solution)/shard_map/pallas_call | solution.py:560
  15.6 0.0 collective-permute-done.next_couple
  15.6 0.0 copy-done.1
  15.6 4.3 %shard_map.78 = (f32[4,4,64,128]{3,2,1,0:T(8,128)S(1)}, f32[4,64,128]{2,1,0:T(8,128)S(1)}) custom-call(s32[1]{0:T(128)} %bitcast.slab, f32[256,256]{1,0:T(8,128)S(1)} %get-tuple-element.13.s, f32[2,1,64,64]{3,2,1,0:T(8,128)S(1)} %copy-done.1, f32[2,1,64,64]{3,2,1,0:T(8,128)S(1)} %collective-permute-done.next_couple), custom_call_target="tpu_custom_call" | custom-call | flops 5500000256 | bytes 1048576 | tf_op jit(solution)/shard_map/pallas_call | solution.py:561
  19.9 11.6 %all_to_all.15.near = f32[4,4,64,128]{3,2,1,0:T(8,128)S(1)} all-to-all(f32[4,4,64,128]{3,2,1,0:T(8,128)S(1)} %get-tuple-element.14), channel_id=1, replica_groups={{0,2,4,6},{1,3,5,7},{8,10,12,14},{9,11,13,15},{16,18,20,22},{17,19,21,2..., dimensions={0} | all-to-all | bytes 1048576 | tf_op jit(solution)/shard_map/all_to_all | solution.py:562
  31.5 3.1 %collective-permute-start.1 = (f32[4,4,64,128]{3,2,1,0:T(8,128)S(1)}, f32[4,4,64,128]{3,2,1,0:T(8,128)S(1)}, u32[]{:S(2)}, u32[]{:S(2)}) collective-permute-start(f32[4,4,64,128]{3,2,1,0:T(8,128)S(1)} %all_to_all.15.near), channel_id=1, source_target_pairs={{0,1},{1,0},{2,3},{3,2},{4,5},{5,4},{6,7},{7,6},{8,9},{9,8},{10,11... | collective-permute-start | bytes 1572872 | tf_op jit(solution)/shard_map/ppermute | solution.py:565
  34.7 1.5 collective-permute-done.1.far
  36.2 0.7 copy-done.2
  36.9 24.4 %shard_map.79 = (f32[32,2,8,256]{3,2,1,0:T(8,128)}, f32[128,256]{1,0:T(8,128)S(1)}, f32[128,256]{1,0:T(8,128)S(1)}, f32[5,64,128]{2,1,0:T(8,128)S(1)}) custom-call(s32[1]{0:T(128)} %bitcast.slab, f32[2,1,64,64]{3,2,1,0:T(8,128)S(1)} %copy-done.1, f32[2,1,64,64]{3,2,1,0:T(8,128)S(1)} %collective-permute-done.next_couple, f32[1,1,256]{2,1,0:T(1,128)S(1)} %copy-done.2, ...), custom_call_target="tpu_custom_call" | custom-call | flops 27499999232 | bytes 1048576 | tf_op jit(solution)/shard_map/pallas_call | solution.py:566
  61.2 45.9 %all-to-all-start.1 = ((f32[64,8,256]{2,1,0:T(8,128)}), f32[64,8,256]{2,1,0:T(8,128)S(1)}, u32[]{:S(2)}, u32[]{:S(2)}) async-start(f32[64,8,256]{2,1,0:T(8,128)} %bitcast.3), calls=%async_computation.1 | async-start | bytes 1048576 | tf_op jit(solution)/shard_map/all_to_all | solution.py:555
  107.1 1.9 %collective-permute-start.4 = (f32[5,64,128]{2,1,0:T(8,128)S(1)}, f32[5,64,128]{2,1,0:T(8,128)S(1)}, u32[]{:S(2)}, u32[]{:S(2)}) collective-permute-start(f32[5,64,128]{2,1,0:T(8,128)S(1)} %get-tuple-element.19), channel_id=1, source_target_pairs={{0,2},{1,3},{2,4},{3,5},{4,6},{5,7},{6,0},{7,1},{8,10},{9,11},{10,... | collective-permute-start | bytes 491528 | tf_op jit(solution)/shard_map/ppermute | solution.py:579
  109.0 4.7 %collective-permute-start.3 = (f32[5,64,128]{2,1,0:T(8,128)S(1)}, f32[5,64,128]{2,1,0:T(8,128)S(1)}, u32[]{:S(2)}, u32[]{:S(2)}) collective-permute-start(f32[5,64,128]{2,1,0:T(8,128)S(1)} %get-tuple-element.19), channel_id=1, source_target_pairs={{0,4},{1,5},{2,6},{3,7},{4,0},{5,1},{6,2},{7,3},{8,12},{9,13},{10,... | collective-permute-start | bytes 491528 | tf_op jit(solution)/shard_map/ppermute | solution.py:579
  113.7 1.9 %collective-permute-start.2 = (f32[5,64,128]{2,1,0:T(8,128)S(1)}, f32[5,64,128]{2,1,0:T(8,128)S(1)}, u32[]{:S(2)}, u32[]{:S(2)}) collective-permute-start(f32[5,64,128]{2,1,0:T(8,128)S(1)} %get-tuple-element.19), channel_id=1, source_target_pairs={{0,6},{1,7},{2,0},{3,1},{4,2},{5,3},{6,4},{7,5},{8,14},{9,15},{10,... | collective-permute-start | bytes 491528 | tf_op jit(solution)/shard_map/ppermute | solution.py:579
  115.6 0.6 collective-permute-done.4
  116.3 2.8 %collective-permute-done.3 = f32[5,64,128]{2,1,0:T(8,128)S(1)} collective-permute-done((f32[5,64,128]{2,1,0:T(8,128)S(1)}, f32[5,64,128]{2,1,0:T(8,128)S(1)}, u32[]{:S(2)}, u32[]{:S(2)}) %collective-permute-start.3) | collective-permute-done | bytes 163872 | tf_op jit(solution)/shard_map/ppermute | solution.py:579
  119.0 2.2 %collective-permute-done.2 = f32[5,64,128]{2,1,0:T(8,128)S(1)} collective-permute-done((f32[5,64,128]{2,1,0:T(8,128)S(1)}, f32[5,64,128]{2,1,0:T(8,128)S(1)}, u32[]{:S(2)}, u32[]{:S(2)}) %collective-permute-start.2) | collective-permute-done | bytes 163872 | tf_op jit(solution)/shard_map/ppermute | solution.py:579
  121.3 3.4 %collective-permute-start.5 = (f32[4,5,64,128]{3,2,1,0:T(8,128)S(1)}, f32[4,5,64,128]{3,2,1,0:T(8,128)S(1)}, u32[]{:S(2)}, u32[]{:S(2)}) collective-permute-start(f32[4,5,64,128]{3,2,1,0:T(8,128)S(1)} %pad_maximum_fusion.near), channel_id=1, source_target_pairs={{0,1},{1,0},{2,3},{3,2},{4,5},{5,4},{6,7},{7,6},{8,9},{9,8},{10,11... | collective-permute-start | bytes 1966088 | tf_op jit(solution)/shard_map/ppermute | solution.py:581
  124.7 1.7 collective-permute-done.5.far
  126.4 7.5 %shard_map.82 = f32[32,2,8,256]{3,2,1,0:T(8,128)} custom-call(s32[1]{0:T(128)} %bitcast.slab, f32[2,1,64,64]{3,2,1,0:T(8,128)S(1)} %copy-done.1, f32[4,5,64,128]{3,2,1,0:T(8,128)S(1)} %pad_maximum_fusion.near, f32[4,5,64,128]{3,2,1,0:T(8,128)S(1)} %collective-permute-done.5.far, f32[128,256]{1,0:T(8,128)S(1)} %get-tuple-element.22.big, ...), custom_call_target="tpu_custom_call" | custom-call | flops 8800000000 | bytes 1048576 | tf_op jit(solution)/shard_map/pallas_call | solution.py:585
  134.0 0.0 all-to-all-done.1.piece
  134.0 14.8 %all-to-all-start.2 = ((f32[64,8,256]{2,1,0:T(8,128)}), f32[64,8,256]{2,1,0:T(8,128)S(1)}, u32[]{:S(2)}, u32[]{:S(2)}) async-start(f32[64,8,256]{2,1,0:T(8,128)} %bitcast.9), calls=%async_computation.2 | async-start | bytes 1048576 | tf_op jit(solution)/shard_map/all_to_all | solution.py:555
  148.8 0.0 copy-done.3
  148.8 0.1 rev.3
  148.9 0.2 shard_map.80
  149.1 1.3 shard_map.81
  150.4 28.1 %all-to-all-done.2.piece = f32[64,8,256]{2,1,0:T(8,128)S(1)} async-done(((f32[64,8,256]{2,1,0:T(8,128)}), f32[64,8,256]{2,1,0:T(8,128)S(1)}, u32[]{:S(2)}, u32[]{:S(2)}) %all-to-all-start.2) | async-done | bytes 524320 | tf_op jit(solution)/shard_map/all_to_all | solution.py:555
  178.5 1.3 shard_map.83
  (7 shorter events, 0.1 us)
Async XLA Ops:
  0.6 15.0 %collective-permute-start = (f32[2,1,64,64]{3,2,1,0:T(8,128)}, f32[2,1,64,64]{3,2,1,0:T(8,128)S(1)}, u32[]{:S(2)}, u32[]{:S(2)}) collective-permute-start(f32[2,1,64,64]{3,2,1,0:T(8,128)} %couple.5), channel_id=1, source_target_pairs={{0,7},{1,0},{2,1},{3,2},{4,3},{5,4},{6,5},{7,6},{8,15},{9,8},{10,9... | collective-permute-start | bytes 98312 | tf_op jit(solution)/shard_map/ppermute | solution.py:557
  8.2 0.7 copy-start.4
  8.9 1.0 copy-start
  9.9 5.7 %copy-start.1 = (f32[2,1,64,64]{3,2,1,0:T(8,128)S(1)}, f32[2,1,64,64]{3,2,1,0:T(8,128)}, u32[]{:S(2)}) copy-start(f32[2,1,64,64]{3,2,1,0:T(8,128)} %couple.5) | copy-start | bytes 98308
  31.5 4.7 %collective-permute-start.1 = (f32[4,4,64,128]{3,2,1,0:T(8,128)S(1)}, f32[4,4,64,128]{3,2,1,0:T(8,128)S(1)}, u32[]{:S(2)}, u32[]{:S(2)}) collective-permute-start(f32[4,4,64,128]{3,2,1,0:T(8,128)S(1)} %all_to_all.15.near), channel_id=1, source_target_pairs={{0,1},{1,0},{2,3},{3,2},{4,5},{5,4},{6,7},{7,6},{8,9},{9,8},{10,11... | collective-permute-start | bytes 1572872 | tf_op jit(solution)/shard_map/ppermute | solution.py:565
  36.2 0.7 copy-start.2
  61.2 72.8 %all-to-all-start.1 = ((f32[64,8,256]{2,1,0:T(8,128)}), f32[64,8,256]{2,1,0:T(8,128)S(1)}, u32[]{:S(2)}, u32[]{:S(2)}) async-start(f32[64,8,256]{2,1,0:T(8,128)} %bitcast.3), calls=%async_computation.1 | async-start | bytes 1048576 | tf_op jit(solution)/shard_map/all_to_all | solution.py:555
  107.1 9.2 %collective-permute-start.4 = (f32[5,64,128]{2,1,0:T(8,128)S(1)}, f32[5,64,128]{2,1,0:T(8,128)S(1)}, u32[]{:S(2)}, u32[]{:S(2)}) collective-permute-start(f32[5,64,128]{2,1,0:T(8,128)S(1)} %get-tuple-element.19), channel_id=1, source_target_pairs={{0,2},{1,3},{2,4},{3,5},{4,6},{5,7},{6,0},{7,1},{8,10},{9,11},{10,... | collective-permute-start | bytes 491528 | tf_op jit(solution)/shard_map/ppermute | solution.py:579
  109.0 10.0 %collective-permute-start.3 = (f32[5,64,128]{2,1,0:T(8,128)S(1)}, f32[5,64,128]{2,1,0:T(8,128)S(1)}, u32[]{:S(2)}, u32[]{:S(2)}) collective-permute-start(f32[5,64,128]{2,1,0:T(8,128)S(1)} %get-tuple-element.19), channel_id=1, source_target_pairs={{0,4},{1,5},{2,6},{3,7},{4,0},{5,1},{6,2},{7,3},{8,12},{9,13},{10,... | collective-permute-start | bytes 491528 | tf_op jit(solution)/shard_map/ppermute | solution.py:579
  113.7 7.6 %collective-permute-start.2 = (f32[5,64,128]{2,1,0:T(8,128)S(1)}, f32[5,64,128]{2,1,0:T(8,128)S(1)}, u32[]{:S(2)}, u32[]{:S(2)}) collective-permute-start(f32[5,64,128]{2,1,0:T(8,128)S(1)} %get-tuple-element.19), channel_id=1, source_target_pairs={{0,6},{1,7},{2,0},{3,1},{4,2},{5,3},{6,4},{7,5},{8,14},{9,15},{10,... | collective-permute-start | bytes 491528 | tf_op jit(solution)/shard_map/ppermute | solution.py:579
  121.3 5.1 %collective-permute-start.5 = (f32[4,5,64,128]{3,2,1,0:T(8,128)S(1)}, f32[4,5,64,128]{3,2,1,0:T(8,128)S(1)}, u32[]{:S(2)}, u32[]{:S(2)}) collective-permute-start(f32[4,5,64,128]{3,2,1,0:T(8,128)S(1)} %pad_maximum_fusion.near), channel_id=1, source_target_pairs={{0,1},{1,0},{2,3},{3,2},{4,5},{5,4},{6,7},{7,6},{8,9},{9,8},{10,11... | collective-permute-start | bytes 1966088 | tf_op jit(solution)/shard_map/ppermute | solution.py:581
  134.0 14.8 %copy-start.3 = (f32[2,2,127]{2,1,0:T(2,128)S(1)}, f32[2,2,127]{2,1,0:T(2,128)}, u32[]{:S(2)}) copy-start(f32[2,2,127]{2,1,0:T(2,128)} %param.11) | copy-start | bytes 6100
  134.0 44.5 %all-to-all-start.2 = ((f32[64,8,256]{2,1,0:T(8,128)}), f32[64,8,256]{2,1,0:T(8,128)S(1)}, u32[]{:S(2)}, u32[]{:S(2)}) async-start(f32[64,8,256]{2,1,0:T(8,128)} %bitcast.9), calls=%async_computation.2 | async-start | bytes 1048576 | tf_op jit(solution)/shard_map/all_to_all | solution.py:555
